TPU v7x, 256 devices: a whole 4x4x8 slice. The times are simulated.
256 devices in a mesh: grp: 4 (over y_lo, core), doc: 16 (over z, y_hi), col: 4 (over x).
Axes of the slice: x: 4, y: 4 (y_hi: 2, y_lo: 2; y = y_hi * 2 + y_lo), z: 8, core: 2. Of those that a mesh axis runs over, the one named last changes fastest.
Arguments:
- mlp_input: bfloat16 [6144, 4096], P('grp', 'col'), may hold values from -6 to 6
- out_grad: bfloat16 [6144, 4096], P('grp', 'col'), may hold values from -6 to 6
- w_gate: bfloat16 [4096, 14336], P('col', 'doc'), may hold values from -0.09375 to 0.09375
- w_up: bfloat16 [4096, 14336], P('col', 'doc'), may hold values from -0.09375 to 0.09375
- w_down: bfloat16 [14336, 4096], P('doc', 'col'), may hold values from -0.046875 to 0.046875
- proj_down_in: bfloat16 [14336, 64], P('doc'), may hold values from -0.046875 to 0.046875
- proj_down_out: bfloat16 [4096, 64], P('col'), may hold values from -0.09375 to 0.09375
- proj_up_in: bfloat16 [4096, 64], P('col'), may hold values from -0.09375 to 0.09375
- proj_up_out: bfloat16 [14336, 64], P('doc'), may hold values from -0.046875 to 0.046875
- store: bfloat16 [32768, 8192], P(('grp', 'doc'), 'col'), may hold values from -100 to 100
- layer_mask: int32 [32768, 2], P(('grp', 'doc')), may hold values 0 or 1
- live_count: int32 [64], P(('grp', 'doc')), may hold values from 1 to 512, 16384 in all
Outputs:
- scores: float32 [24, 32768], P(None, ('grp', 'doc', 'col'))
Inputs may be any that keep to these rules, and one draw needn't show every extreme that they name: Owner p = grp index * 16 + doc index holds slots p * 512 to p * 512 + 511; the first live_count[p] of them hold documents.
All inputs are finite; a program needn't handle non-finite values. No bound on the sum of `layer_mask` or of `live_count` on one device may be relied on, other than what follows from the above.
Results may differ from a plain program's by a relative error of at most 0.03.
Values may be sent and summed in bfloat16 or wider, within the bound.
A program may use at most 128 MiB of HBM per device.

v0:
```python
import functools
import math

import jax
import jax.numpy as jnp
from jax import lax
from jax.experimental import pallas as pl
from jax.experimental.pallas import tpu as pltpu
from jax.sharding import PartitionSpec as P

MESH = pl.DeviceIdType.MESH
SEQ = 256
LANES = 128
EPSILON = 1e-06
NT = (((1,), (1,)), ((), ()))
f32, bf16 = jnp.float32, jnp.bfloat16


def dot(left, right):
    return jnp.dot(left, right, preferred_element_type=f32)


def dot_nt(left, right):
    return lax.dot_general(left, right, NT, preferred_element_type=f32)


def kernel(
    sizes,
    x_in,
    og_in,
    wg_in,
    wu_in,
    wd_in,
    pdi_in,
    pdo_in,
    pui_in,
    puo_in,
    store_in,
    mask_in,
    live_in,
    out_ref,
    x,
    og,
    wg,
    wu,
    wd,
    pdi,
    pdo,
    pui,
    puo,
    store,
    mask,
    live,
    gate,
    up,
    hg,
    s,
    send_a,
    recv_a,
    send_b,
    recv_b,
    ends_part,
    ends_recv,
    ends,
    ends_t,
    ui2,
    pairs,
    grads,
    grads_send,
    x_recv,
    block,
    block_send,
    z_recv,
    y_send,
    y_recv,
    full,
    norm_send,
    norm_recv,
    c_send,
    c_recv,
    load_sem,
    x_load_sem,
    ring_s,
    ring_r,
    ends_s,
    ends_r,
    gather_s,
    gather_r,
    pair_s,
    pair_r,
    x_s,
    x_r,
    z_s,
    z_r,
    y_s,
    y_r,
    norm_s,
    norm_r,
    c_s,
    c_r,
):
    n_grp, n_doc, n_col, nq = sizes
    part = SEQ // n_col
    half = part // 2
    early = nq // 2
    batches = ((0, early), (early, nq - 1 - early), (nq - 1, 1))
    g, d, c = lax.axis_index("grp"), lax.axis_index("doc"), lax.axis_index("col")
    right, left, across = (
        lax.rem(c + 1, n_col),
        lax.rem(c + n_col - 1, n_col),
        lax.rem(c + 2, n_col),
    )
    n_z = n_doc // 2
    z, upper_y = d // 2, lax.rem(d, 2)
    k_dim = pdi_in.shape[0]

    def along_z(k):
        return {"doc": lax.rem(z + k, n_z) * 2 + upper_y}

    def along_y(j, e):
        return {"grp": lax.rem(g + j, n_grp), "doc": z * 2 + (upper_y + e - 2 * upper_y * e)}

    x_steps = sorted(range(1, n_col), key=lambda k: -min(k, n_col - k))
    z_steps = sorted(range(1, n_z), key=lambda k: -min(k, n_z - k))
    y_steps = [(j, e) for e in (1, 0) for j in range(n_grp) if j or e]

    def remote(src, dst, send, recv, **place):
        return pltpu.make_async_remote_copy(
            src_ref=src,
            dst_ref=dst,
            send_sem=send,
            recv_sem=recv,
            device_id=place,
            device_id_type=MESH,
        )

    def token_rows(p):
        return pl.ds(pl.multiple_of(p * SEQ, SEQ), SEQ)

    def own_rows(owner, first, count):
        return pl.ds(pl.multiple_of(owner * part + first, half), count)

    loads = {}

    def load(key, src, dst):
        copy = pltpu.make_async_copy(src, dst, load_sem.at[len(loads)])
        copy.start()
        loads[key] = copy

    def x_load(p):
        return pltpu.make_async_copy(
            x_in.at[token_rows(p)], x.at[token_rows(p)], x_load_sem.at[p]
        )

    load("wg", wg_in, wg)
    x_load(0).start()

    barrier = pltpu.get_barrier_semaphore()

    def greet(place):
        pl.semaphore_signal(barrier, 1, device_id=place, device_id_type=MESH)

    for k in z_steps:
        greet(along_z(k))
    for j, e in y_steps:
        greet(along_y(j, e))
    for k in x_steps:
        greet({"col": lax.rem(c + k, n_col)})
    for p in range(1, nq):
        x_load(p).start()

    loads["wg"].wait()
    x_load(0).wait()
    load("og", og_in, og)
    load("pdo", pdo_in, pdo.at[pl.ds(0, k_dim)])
    load("pui", pui_in, pui.at[pl.ds(k_dim, k_dim)])
    load("wu", wu_in, wu)
    load("wd", wd_in, wd)
    load("store", store_in, store)
    load("mask", mask_in, mask)
    load("pdi", pdi_in, pdi.at[pl.ds(0, k_dim)])
    load("pdi2", pdi_in, pdi.at[pl.ds(k_dim, k_dim)])
    load("puo", puo_in, puo)
    load("live", live_in, live)

    def gate_term(p):
        gate[p] = dot(x[token_rows(p)], wg[...])
        send_a[p] = gate[p, own_rows(across, 0, part)].astype(bf16)

    gate_term(0)
    pl.semaphore_wait(barrier, n_z - 1 + len(y_steps) + n_col - 1)

    def copy_a(p, way):
        rows = pl.ds(way * half, half)
        return remote(
            send_a.at[p, rows],
            recv_a.at[p, way],
            ring_s.at[0, p, way],
            ring_r.at[0, p, way],
            col=(right, left)[way],
        )

    def copy_b(p, way):
        return remote(
            send_b.at[p, way],
            recv_b.at[p, way],
            ring_s.at[1, p, way],
            ring_r.at[1, p, way],
            col=(right, left)[way],
        )

    def copy_g(p, way, slot):
        return remote(
            s.at[p, slot],
            s.at[p, slot],
            ring_s.at[2, p, way],
            ring_r.at[2, p, way],
            col=(right, left)[way],
        )

    def copy_f(p, way, slot):
        rows = pl.ds(way * half, half)
        return remote(
            s.at[p, slot, rows],
            s.at[p, slot, rows],
            ring_s.at[3, p, way],
            ring_r.at[3, p, way],
            col=(right, left)[way],
        )

    copy_a(0, 0).start()
    copy_a(0, 1).start()

    def gate_step(p, carry):
        x_load(p).wait()
        gate_term(p)
        copy_a(p, 0).start()
        copy_a(p, 1).start()
        return carry

    lax.fori_loop(1, nq, gate_step, 0)

    slab = ends_part.shape[0]
    loads["og"].wait()
    loads["pdo"].wait()
    loads["pui"].wait()
    pdo[pl.ds(k_dim, k_dim)] = jnp.zeros((k_dim, pdo.shape[1]), bf16)
    pui[pl.ds(0, k_dim)] = jnp.zeros((k_dim, pui.shape[1]), bf16)
    mine = pl.ds(pl.multiple_of((upper_y * n_z + z) * slab, slab), slab)
    ends_part[...] = (dot_nt(og[mine], pdo[...]) + dot_nt(x[mine], pui[...])).astype(bf16)

    def copy_ends(k):
        return remote(
            ends_part,
            ends_recv.at[k - 1],
            ends_s.at[k - 1],
            ends_r.at[k - 1],
            col=lax.rem(c + k, n_col),
        )

    for k in range(1, n_col):
        copy_ends(k).start()

    loads["wu"].wait()
    loads["wd"].wait()

    def terms_step(p, carry):
        up[p] = dot(x[token_rows(p)], wu[...]).astype(bf16)
        copy_a(p, 0).wait_recv()
        send_b[p, 0, pl.ds(0, half)] = (
            gate[p, own_rows(right, 0, half)] + recv_a[p, 0].astype(f32)
        ).astype(bf16)
        send_b[p, 0, pl.ds(half, half)] = gate[p, own_rows(right, half, half)].astype(bf16)
        copy_b(p, 0).start()
        copy_a(p, 1).wait_recv()
        send_b[p, 1, pl.ds(0, half)] = gate[p, own_rows(left, 0, half)].astype(bf16)
        send_b[p, 1, pl.ds(half, half)] = (
            gate[p, own_rows(left, half, half)] + recv_a[p, 1].astype(f32)
        ).astype(bf16)
        copy_b(p, 1).start()
        hg[p] = dot_nt(og[token_rows(p)], wd[...]).astype(bf16)
        return carry

    lax.fori_loop(0, nq, terms_step, 0)

    for k in range(1, n_col):
        copy_ends(k).wait_recv()
    total = ends_part[...].astype(f32)
    for k in range(1, n_col):
        total += ends_recv[k - 1].astype(f32)
    ends[mine] = total.astype(bf16)

    def copy_gather(k, owner):
        rows = pl.ds(pl.multiple_of((upper_y * n_z + owner) * slab, slab), slab)
        return remote(
            ends.at[rows],
            ends.at[rows],
            gather_s.at[k - 1],
            gather_r.at[k - 1],
            **along_z(k),
        )

    def copy_pair(owner):
        rows = pl.ds(pl.multiple_of(owner * n_z * slab, n_z * slab), n_z * slab)
        return remote(ends.at[rows], ends.at[rows], pair_s, pair_r, **along_y(0, 1))

    for k in range(1, n_z):
        copy_gather(k, z).start()

    loads["store"].wait()
    squares = jnp.zeros((store.shape[0], LANES), f32)
    for j in range(store.shape[1] // LANES):
        value = store[:, pl.ds(j * LANES, LANES)].astype(f32)
        squares += value * value
    upper = squares.astype(bf16)
    lower = (squares - upper.astype(f32)).astype(bf16)
    ones = jnp.ones((8, LANES), bf16)
    doc_squares = dot_nt(ones, upper) + dot_nt(ones, lower)
    loads["mask"].wait()
    keep = jnp.where(c < n_col // 2, mask[0:1, :], mask[1:2, :]).astype(f32)
    doc_squares = doc_squares * keep
    out_width = store.shape[0] // n_col
    for j in range(n_col):
        norm_send[j] = doc_squares[:, j * out_width : (j + 1) * out_width]

    def copy_norm(k):
        to = lax.rem(c + k, n_col)
        return remote(
            norm_send.at[to], norm_recv.at[k - 1], norm_s.at[k - 1], norm_r.at[k - 1], col=to
        )

    def own_step(p, carry):
        copy_b(p, 0).wait_recv()
        copy_b(p, 1).wait_recv()
        value = (
            gate[p, own_rows(c, 0, part)] + recv_b[p, 0].astype(f32) + recv_b[p, 1].astype(f32)
        )
        s[p, c] = (value * jax.nn.sigmoid(value)).astype(bf16)
        copy_g(p, 0, c).start()
        copy_g(p, 1, c).start()
        return carry

    def forward_step(p, carry):
        copy_g(p, 0, left).wait_recv()
        copy_f(p, 0, left).start()
        copy_g(p, 1, right).wait_recv()
        copy_f(p, 1, right).start()
        return carry

    lax.fori_loop(0, early, own_step, 0)
    for k in range(1, n_col):
        copy_norm(k).start()

    n_query = n_grp * nq
    n_sub = x_recv.shape[2]
    for k in range(1, n_z):
        copy_gather(k, lax.rem(z + n_z - k, n_z)).wait_recv()
    copy_pair(upper_y).start()
    lax.fori_loop(0, early - 1, forward_step, 0)
    copy_pair(1 - upper_y).wait_recv()
    low_lanes = lax.broadcasted_iota(jnp.int32, (SEQ, LANES), 1) < k_dim

    def ends_step(p, carry):
        value = ends[token_rows(p)].astype(f32)
        ends_t[p] = value.T[:k_dim].astype(bf16)
        ui2[p] = jnp.where(low_lanes, pltpu.roll(value, k_dim, 1), value).astype(bf16)
        return carry

    lax.fori_loop(0, nq, ends_step, 0)

    lax.fori_loop(early, early + 1, own_step, 0)
    lax.fori_loop(early - 1, early, forward_step, 0)
    lax.fori_loop(early + 1, nq, own_step, 0)

    loads["pdi"].wait()
    loads["pdi2"].wait()
    loads["puo"].wait()
    low_half = lax.broadcasted_iota(jnp.int32, (k_dim // 2, LANES), 1) < k_dim

    def grads_step(p, carry):
        copy_f(p, 0, across).wait_recv()
        copy_f(p, 1, across).wait_recv()
        shared = s[p].reshape(SEQ, s.shape[-1])
        down_in = dot_nt(up[p] * shared, pdi[...])
        up_out = dot_nt(puo[...], hg[p] * shared)
        pairs[pl.ds(0, k_dim)] = dot(ends_t[p], down_in.astype(bf16))
        pairs[pl.ds(k_dim, k_dim)] = dot(up_out.astype(bf16), ui2[p])
        for m in range(2):
            even = pairs[pl.ds(m * k_dim, k_dim // 2, 2)]
            odd = pairs[pl.ds(m * k_dim + 1, k_dim // 2, 2)]
            value = jnp.where(low_half, even, odd)
            grads[p, pl.ds(m * (k_dim // 2), k_dim // 2)] = value
            grads_send[p, pl.ds(m * (k_dim // 2), k_dim // 2)] = value.astype(bf16)
        return carry

    def copy_x(batch, k):
        first, count = batches[batch]
        to = lax.rem(c + k, n_col)
        return remote(
            grads_send.at[
                pl.ds(first, count), pl.ds(pl.multiple_of(to * n_sub, n_sub), n_sub)
            ],
            x_recv.at[k - 1, pl.ds(first, count)],
            x_s.at[batch, k - 1],
            x_r.at[batch, k - 1],
            col=to,
        )

    def copy_z(batch, k):
        first, count = batches[batch]
        return remote(
            block_send.at[pl.ds(first, count)],
            z_recv.at[k - 1, pl.ds(first, count)],
            z_s.at[batch, k - 1],
            z_r.at[batch, k - 1],
            **along_z(k),
        )

    def copy_y(batch, j, e):
        first, count = batches[batch]
        return remote(
            y_send.at[pl.ds(first, count)],
            y_recv.at[j, e, pl.ds(first, count)],
            y_s.at[batch, j, e],
            y_r.at[batch, j, e],
            **along_y(j, e),
        )

    def make_grads(batch):
        first, count = batches[batch]
        lax.fori_loop(first, first + count, grads_step, 0)
        for k in x_steps:
            copy_x(batch, k).start()

    def sum_col(batch):
        first, count = batches[batch]
        span = pl.ds(first, count)
        for k in range(1, n_col):
            copy_x(batch, k).wait_recv()
        total = grads[span, pl.ds(pl.multiple_of(c * n_sub, n_sub), n_sub)]
        for k in range(1, n_col):
            total += x_recv[k - 1, span].astype(f32)
        block[span] = total
        block_send[span] = total.astype(bf16)

        for k in z_steps:
            copy_z(batch, k).start()

    def sum_z(batch):
        first, count = batches[batch]
        span = pl.ds(first, count)

        for k in range(1, n_z):
            copy_z(batch, k).wait_recv()
        total = block[span]
        for k in range(1, n_z):
            total += z_recv[k - 1, span].astype(f32)
        block[span] = total
        y_send[span] = total.astype(bf16)
        for j, e in y_steps:
            copy_y(batch, j, e).start()

    def sum_y(batch):
        first, count = batches[batch]
        span = pl.ds(first, count)
        for j in range(n_grp):
            copy_y(batch, j, 1).wait_recv()
            if j:
                copy_y(batch, j, 0).wait_recv()
                total = y_recv[j, 0, span].astype(f32)
            else:
                total = block[span]
            total += y_recv[j, 1, span].astype(f32)
            for q in range(count):
                row = lax.rem(g + n_grp - j, n_grp) * nq + first + q
                full[pl.ds(row, n_sub, n_query), :] = total[q]

    make_grads(0)
    lax.fori_loop(early, nq, forward_step, 0)
    sum_col(0)
    make_grads(1)
    make_grads(2)
    sum_col(1)
    sum_z(0)
    sum_col(2)
    sum_z(1)
    sum_y(0)
    sum_z(2)
    sum_y(1)
    sum_y(2)

    query = jnp.concatenate(
        [full[pl.ds(kk * n_query, n_query), :] for kk in range(n_sub)], axis=1
    )
    raw = dot_nt(query.astype(bf16), store[...]) * keep
    query_squares = jnp.broadcast_to(
        jnp.sum(query * query, axis=1, keepdims=True), (n_query, out_width)
    )
    for j in range(n_col):
        c_send[j] = jnp.concatenate(
            [raw[:, j * out_width : (j + 1) * out_width], query_squares], axis=0
        ).astype(bf16)

    def copy_c(k):
        to = lax.rem(c + k, n_col)
        return remote(c_send.at[to], c_recv.at[k - 1], c_s.at[k - 1], c_r.at[k - 1], col=to)

    for k in x_steps:
        copy_c(k).start()
    def ring_done(p, carry):
        for way in range(2):
            copy_a(p, way).wait_send()
            copy_b(p, way).wait_send()
            copy_g(p, way, c).wait_send()
            copy_f(p, way, left).wait_send()
        return carry

    lax.fori_loop(0, nq, ring_done, 0)

    for k in range(1, n_z):
        copy_gather(k, z).wait_send()
        for batch in range(len(batches)):
            copy_z(batch, k).wait_send()
    copy_pair(upper_y).wait_send()
    for k in range(1, n_col):
        copy_ends(k).wait_send()
        copy_norm(k).wait_send()
        for batch in range(len(batches)):
            copy_x(batch, k).wait_send()
    for j, e in y_steps:
        for batch in range(len(batches)):
            copy_y(batch, j, e).wait_send()
    norms = norm_send[c]
    for k in range(1, n_col):
        copy_norm(k).wait_recv()
        norms += norm_recv[k - 1]
    columns = float(n_col * n_sub * LANES)
    doc_norm = jnp.sqrt(norms[0:1] / columns + EPSILON) * math.sqrt(columns)
    total = c_send[c].astype(f32)
    for k in range(1, n_col):
        copy_c(k).wait_recv()
    for k in range(1, n_col):
        total += c_recv[k - 1].astype(f32)
    query_norm = jnp.sqrt(total[n_query:] / columns + EPSILON)
    scores = total[:n_query] / (query_norm * doc_norm)
    slot = c * out_width + lax.broadcasted_iota(jnp.int32, scores.shape, 1)
    loads["live"].wait()
    out_ref[...] = jnp.where(slot < live[0], scores, 0.0)
    for k in x_steps:
        copy_c(k).wait_send()


def local(
    mlp_input,
    out_grad,
    w_gate,
    w_up,
    w_down,
    proj_down_in,
    proj_down_out,
    proj_up_in,
    proj_up_out,
    store,
    layer_mask,
    live_count,
):
    n_grp, n_doc, n_col = (lax.axis_size(name) for name in ("grp", "doc", "col"))
    tokens, depth = mlp_input.shape
    width = w_gate.shape[1]
    k_dim = proj_down_in.shape[1]
    nq = tokens // SEQ
    part = SEQ // n_col
    slab = tokens // n_doc
    n_row = 2 * k_dim * k_dim // LANES
    n_sub = n_row // n_col
    out_width = store.shape[0] // n_col
    dma = pltpu.SemaphoreType.DMA
    scratch = [
        pltpu.VMEM((tokens, depth), bf16),
        pltpu.VMEM((tokens, depth), bf16),
        pltpu.VMEM((depth, width), bf16),
        pltpu.VMEM((depth, width), bf16),
        pltpu.VMEM((width, depth), bf16),
        pltpu.VMEM((2 * k_dim, width), bf16),
        pltpu.VMEM((2 * k_dim, depth), bf16),
        pltpu.VMEM((2 * k_dim, depth), bf16),
        pltpu.VMEM((k_dim, width), bf16),
        pltpu.VMEM(store.shape, bf16),
        pltpu.VMEM(layer_mask.shape[::-1], jnp.int32),
        pltpu.SMEM(live_count.shape, jnp.int32),
        pltpu.VMEM((nq, SEQ, width), f32),
        pltpu.VMEM((nq, SEQ, width), bf16),
        pltpu.VMEM((nq, SEQ, width), bf16),
        pltpu.VMEM((nq, n_col, part, width), bf16),
        pltpu.VMEM((nq, part, width), bf16),
        pltpu.VMEM((nq, 2, part // 2, width), bf16),
        pltpu.VMEM((nq, 2, part, width), bf16),
        pltpu.VMEM((nq, 2, part, width), bf16),
        pltpu.VMEM((slab, LANES), bf16),
        pltpu.VMEM((n_col - 1, slab, LANES), bf16),
        pltpu.VMEM((tokens, LANES), bf16),
        pltpu.VMEM((nq, k_dim, SEQ), bf16),
        pltpu.VMEM((nq, SEQ, LANES), bf16),
        pltpu.VMEM((2 * k_dim + 8, LANES), f32),
        pltpu.VMEM((nq, n_row, LANES), f32),
        pltpu.VMEM((nq, n_row, LANES), bf16),
        pltpu.VMEM((n_col - 1, nq, n_sub, LANES), bf16),
        pltpu.VMEM((nq, n_sub, LANES), f32),
        pltpu.VMEM((nq, n_sub, LANES), bf16),
        pltpu.VMEM((n_doc // 2 - 1, nq, n_sub, LANES), bf16),
        pltpu.VMEM((nq, n_sub, LANES), bf16),
        pltpu.VMEM((n_grp, 2, nq, n_sub, LANES), bf16),
        pltpu.VMEM(((n_sub + 1) * n_grp * nq, LANES), f32),
        pltpu.VMEM((n_col, 8, out_width), f32),
        pltpu.VMEM((n_col - 1, 8, out_width), f32),
        pltpu.VMEM((n_col, 2 * n_grp * nq, out_width), bf16),
        pltpu.VMEM((n_col - 1, 2 * n_grp * nq, out_width), bf16),
        dma((12,)),
        dma((nq,)),
        dma((4, nq, 2)),
        dma((4, nq, 2)),
        dma((n_col - 1,)),
        dma((n_col - 1,)),
        dma((n_doc // 2 - 1,)),
        dma((n_doc // 2 - 1,)),
        dma(()),
        dma(()),
        dma((3, n_col - 1)),
        dma((3, n_col - 1)),
        dma((3, n_doc // 2 - 1)),
        dma((3, n_doc // 2 - 1)),
        dma((3, n_grp, 2)),
        dma((3, n_grp, 2)),
        dma((n_col - 1,)),
        dma((n_col - 1,)),
        dma((n_col - 1,)),
        dma((n_col - 1,)),
    ]
    scores = pl.pallas_call(
        functools.partial(kernel, (n_grp, n_doc, n_col, nq)),
        out_shape=jax.ShapeDtypeStruct((n_grp * nq, out_width), f32),
        in_specs=[pl.BlockSpec(memory_space=pl.ANY)] * 12,
        out_specs=pl.BlockSpec(memory_space=pltpu.VMEM),
        scratch_shapes=scratch,
        compiler_params=pltpu.CompilerParams(
            collective_id=0, has_side_effects=True, vmem_limit_bytes=58 * 1024 * 1024
        ),
        cost_estimate=pl.CostEstimate(
            flops=6 * tokens * depth * width, bytes_accessed=14 << 20, transcendentals=0
        ),
    )(
        mlp_input,
        out_grad,
        w_gate,
        w_up,
        w_down,
        proj_down_in.T,
        proj_down_out.T,
        proj_up_in.T,
        proj_up_out.T,
        store,
        layer_mask.T,
        live_count,
    )
    return scores


def solution(mesh):
    return jax.shard_map(
        local,
        mesh=mesh,
        in_specs=(
            P("grp", "col"),
            P("grp", "col"),
            P("col", "doc"),
            P("col", "doc"),
            P("doc", "col"),
            P("doc", None),
            P("col", None),
            P("col", None),
            P("doc", None),
            P(("grp", "doc"), "col"),
            P(("grp", "doc"), None),
            P(("grp", "doc")),
        ),
        out_specs=P(None, ("grp", "doc", "col")),
        check_vma=False,
    )
```

profile of v0, /device:TPU:1, one launch (start us, length us, event | category | flops | bytes accessed | tf_op | source)
XLA Modules:
  0.0 78.9 jit_solution(4466595519899022657)
XLA Ops:
  0.7 76.9 %shard_map.118 = f32[24,128]{1,0:T(8,128)} custom-call(bf16[1536,1024]{1,0:T(8,128)(2,1)} %x_in.1, bf16[1536,1024]{1,0:T(8,128)(2,1)} %og_in.1, bf16[1024,896]{1,0:T(8,128)(2,1)} %wg_in.1, bf16[1024,896]{1,0:T(8,128)(2,1)} %wu_in.1, bf16[896,1024]{1,0:T(8,128)(2,1)} %wd_in.1, bf16[64,896]{1,0:T(8,128)(2,1)} %bitcast.7, bf16[64,1024]{1,0:T(8,128)(2,1)} %bitcast.5, ...), custom_call_target="tpu_custom_call" | custom-call | flops 8455716864 | bytes 14680064 | tf_op jit(solution)/shard_map/pallas_call | solution.py:639
  77.6 1.3 %copy.15 = f32[24,128]{1,0:T(8,128)} copy(f32[24,128]{1,0:T(8,128)} %shard_map.118) | data formatting | bytes 24576
where the time goes:
time: 79.1 us; the launch traced here: 78.9 us
  Pallas kernels  76.9 us (97%)
  local copies, waits for them, and re-layouts  1.31 us (2%)
    pallas_call x1, Pallas kernels, local(): pl.pallas_call(functools.partial(kernel, (n_grp, n_doc, n_col, nq)), out_...  76.9 us

commit v1 on v0

--- a/solution.py
+++ b/solution.py
@@ -187,7 +187,8 @@
         gate[p] = dot(x[token_rows(p)], wg[...])
         send_a[p] = gate[p, own_rows(across, 0, part)].astype(bf16)
 
-    gate_term(0)
+    first_rows = pl.ds(pl.multiple_of(across * part, part), part)
+    send_a[0] = dot(x[first_rows], wg[...]).astype(bf16)
     pl.semaphore_wait(barrier, n_z - 1 + len(y_steps) + n_col - 1)
 
     def copy_a(p, way):
@@ -239,6 +240,7 @@
         return carry
 
     lax.fori_loop(1, nq, gate_step, 0)
+    gate[0] = dot(x[token_rows(0)], wg[...])
 
     slab = ends_part.shape[0]
     loads["og"].wait()

time: 79.1 us -> 78.8 us (level)
  no operation moved by 1% of the time
where the time goes in v1:
time: 78.8 us; the launch traced here: 78.6 us
  Pallas kernels  76.6 us (97%)
  local copies, waits for them, and re-layouts  1.31 us (2%)
    pallas_call x1, Pallas kernels, local(): pl.pallas_call(functools.partial(kernel, (n_grp, n_doc, n_col, nq)), out_...  76.6 us

profile of v1, /device:TPU:1, one launch (start us, length us, event | category | flops | bytes accessed | tf_op | source)
XLA Modules:
  0.0 78.6 jit_solution(11097815445151813597)
XLA Ops:
  0.7 76.6 %shard_map.118 = f32[24,128]{1,0:T(8,128)} custom-call(bf16[1536,1024]{1,0:T(8,128)(2,1)} %x_in.1, bf16[1536,1024]{1,0:T(8,128)(2,1)} %og_in.1, bf16[1024,896]{1,0:T(8,128)(2,1)} %wg_in.1, bf16[1024,896]{1,0:T(8,128)(2,1)} %wu_in.1, bf16[896,1024]{1,0:T(8,128)(2,1)} %wd_in.1, bf16[64,896]{1,0:T(8,128)(2,1)} %bitcast.7, bf16[64,1024]{1,0:T(8,128)(2,1)} %bitcast.5, ...), custom_call_target="tpu_custom_call" | custom-call | flops 8455716864 | bytes 14680064 | tf_op jit(solution)/shard_map/pallas_call | solution.py:641
  77.3 1.3 %copy.15 = f32[24,128]{1,0:T(8,128)} copy(f32[24,128]{1,0:T(8,128)} %shard_map.118) | data formatting | bytes 24576

commit v2 on v1

--- a/solution.py
+++ b/solution.py
@@ -494,21 +494,25 @@
     query = jnp.concatenate(
         [full[pl.ds(kk * n_query, n_query), :] for kk in range(n_sub)], axis=1
     )
-    raw = dot_nt(query.astype(bf16), store[...]) * keep
     query_squares = jnp.broadcast_to(
         jnp.sum(query * query, axis=1, keepdims=True), (n_query, out_width)
     )
-    for j in range(n_col):
-        c_send[j] = jnp.concatenate(
-            [raw[:, j * out_width : (j + 1) * out_width], query_squares], axis=0
-        ).astype(bf16)
+    query = query.astype(bf16)
+
+    def scores_for(owner):
+        docs = pl.ds(pl.multiple_of(owner * out_width, out_width), out_width)
+        kept = jnp.where(c < n_col // 2, mask[0:1, docs], mask[1:2, docs]).astype(f32)
+        raw = dot_nt(query, store[docs, :]) * kept
+        return jnp.concatenate([raw, query_squares], axis=0).astype(bf16)
 
     def copy_c(k):
         to = lax.rem(c + k, n_col)
         return remote(c_send.at[to], c_recv.at[k - 1], c_s.at[k - 1], c_r.at[k - 1], col=to)
 
     for k in x_steps:
+        c_send[lax.rem(c + k, n_col)] = scores_for(lax.rem(c + k, n_col))
         copy_c(k).start()
+    total = scores_for(c).astype(f32)
     def ring_done(p, carry):
         for way in range(2):
             copy_a(p, way).wait_send()
@@ -538,7 +542,6 @@
         norms += norm_recv[k - 1]
     columns = float(n_col * n_sub * LANES)
     doc_norm = jnp.sqrt(norms[0:1] / columns + EPSILON) * math.sqrt(columns)
-    total = c_send[c].astype(f32)
     for k in range(1, n_col):
         copy_c(k).wait_recv()
     for k in range(1, n_col):

time: 78.8 us -> 79 us (level)
  no operation moved by 1% of the time
where the time goes in v2:
time: 79 us; the launch traced here: 78.8 us
  Pallas kernels  76.8 us (97%)
  local copies, waits for them, and re-layouts  1.31 us (2%)
    pallas_call x1, Pallas kernels, local(): pl.pallas_call(functools.partial(kernel, (n_grp, n_doc, n_col, nq)), out_...  76.8 us

profile of v2, /device:TPU:1, one launch (start us, length us, event | category | flops | bytes accessed | tf_op | source)
XLA Modules:
  0.0 78.8 jit_solution(4990223175670119545)
XLA Ops:
  0.7 76.8 %shard_map.118 = f32[24,128]{1,0:T(8,128)} custom-call(bf16[1536,1024]{1,0:T(8,128)(2,1)} %x_in.1, bf16[1536,1024]{1,0:T(8,128)(2,1)} %og_in.1, bf16[1024,896]{1,0:T(8,128)(2,1)} %wg_in.1, bf16[1024,896]{1,0:T(8,128)(2,1)} %wu_in.1, bf16[896,1024]{1,0:T(8,128)(2,1)} %wd_in.1, bf16[64,896]{1,0:T(8,128)(2,1)} %bitcast.7, bf16[64,1024]{1,0:T(8,128)(2,1)} %bitcast.5, ...), custom_call_target="tpu_custom_call" | custom-call | flops 8455716864 | bytes 14680064 | tf_op jit(solution)/shard_map/pallas_call | solution.py:644
  77.5 1.3 %copy.15 = f32[24,128]{1,0:T(8,128)} copy(f32[24,128]{1,0:T(8,128)} %shard_map.118) | data formatting | bytes 24576
